TPU v7x, 128 devices: a whole 4x4x4 slice. The times are simulated.
128 devices in a mesh: row: 16 (over x, z), col: 8 (over y, core).
Axes of the slice: x: 4, y: 4, z: 4, core: 2. Of those that a mesh axis runs over, the one named last changes fastest.
Arguments:
- winter: bfloat16 [256, 256, 1024], P(None, 'row', 'col'), may hold values from -6 to 6
- summer: bfloat16 [256, 256, 1024], P(None, 'row', 'col'), may hold values from -6 to 6
- offsets: int32 [2, 16, 8], replicated, may hold values from -1 to 1, as said below
- feat_weight: bfloat16 [256, 2304], replicated, may hold values from -0.125 to 0.125
- bn_gain: float32 [81], replicated, may hold values from 0.5 to 1.5
- bn_shift: float32 [81], replicated, may hold values from -3 to 3
- w_first: bfloat16 [64, 729], replicated, may hold values from -0.21875 to 0.21875
- w_second: bfloat16 [32, 576], replicated, may hold values from -0.25 to 0.25
- cotangent: bfloat16 [32, 256, 1024], P(None, 'row', 'col'), may hold values from -6 to 6
Outputs:
- refined: bfloat16 [32, 256, 1024], P(None, 'row', 'col')
- grad_winter: bfloat16 [256, 256, 1024], P(None, 'row', 'col')
- grad_summer: bfloat16 [256, 256, 1024], P(None, 'row', 'col')
- grad_feat: float32 [256, 2304], replicated
- grad_first: float32 [64, 729], replicated
- grad_second: float32 [32, 576], replicated
- grad_gain: float32 [81], replicated
- grad_shift: float32 [81], replicated
Inputs may be any that keep to these rules, and one draw needn't show every extreme that they name: `offsets`: each offset keeps the summer tile inside the scene.
All inputs are finite; a program needn't handle non-finite values.
Results may differ from a plain program's by a relative error of at most 0.02.
Values may be sent and summed in bfloat16 or wider, within the bound.
A program may use at most 384 MiB of HBM per device.

v0:
```python
import math

import jax
import jax.numpy as jnp
from jax import lax
from jax.sharding import PartitionSpec as P

RADIUS = 4


def extended(block, sides, width):
    for axis, dim in sides:
        count = lax.axis_size(axis)
        forward = [(i, i + 1) for i in range(count - 1)]
        backward = [(target, source) for source, target in forward]
        low = lax.ppermute(
            lax.slice_in_dim(block, block.shape[dim] - width, None, axis=dim), axis, forward
        )
        high = lax.ppermute(lax.slice_in_dim(block, 0, width, axis=dim), axis, backward)
        block = jnp.concatenate([low, block, high], axis=dim)
    return block


def shifted(block, axis, distance):
    devices = range(lax.axis_size(axis))
    route = [(i - distance, i) for i in devices if i - distance in devices]
    return lax.ppermute(block, axis, route)


def silu_slope(value):
    sigma = jax.nn.sigmoid(value)
    return sigma * (1.0 + value * (1.0 - sigma))


def patches(padded, height, wide_cols):
    return jnp.concatenate(
        [
            padded[:, shift_row : shift_row + height, shift_col : shift_col + wide_cols]
            for shift_row in range(3)
            for shift_col in range(3)
        ],
        0,
    ).reshape(-1, height * wide_cols)


def conv_local(padded, weight):
    height = padded.shape[1] - 2
    wide_cols = padded.shape[2] - 2
    output = jnp.dot(weight, patches(padded, height, wide_cols), preferred_element_type=jnp.float32)
    return output.reshape(weight.shape[0], height, wide_cols)


def weight_term(grad, padded):
    out_channels, height, wide_cols = grad.shape
    return lax.dot_general(
        grad.reshape(out_channels, height * wide_cols),
        patches(padded, height, wide_cols),
        (((1,), (1,)), ((), ())),
        preferred_element_type=jnp.float32,
    )


def flip_weight(weight, in_channels):
    out_channels = weight.shape[0]
    return (
        weight.reshape(out_channels, 9, in_channels)[:, ::-1, :]
        .transpose(2, 1, 0)
        .reshape(in_channels, 9 * out_channels)
    )


def correlate(winter_tile, matched):
    channels, height, tile_cols = winter_tile.shape
    disp_side = 2 * RADIUS + 1
    wide_cols = tile_cols + 2 * RADIUS
    corr_scale = 1.0 / math.sqrt(channels)
    pieces = []
    for row_shift in range(disp_side):
        strip_rows = matched[:, row_shift : row_shift + height, :]
        products = jnp.einsum(
            "cij,cim->ijm", winter_tile, strip_rows, preferred_element_type=jnp.float32
        )
        flattened = jnp.pad(
            products.reshape(height, tile_cols * wide_cols), ((0, 0), (0, tile_cols))
        )
        band_cut = flattened.reshape(height, tile_cols, wide_cols + 1)[:, :, :disp_side]
        pieces.append(band_cut.transpose(2, 0, 1))
    return jnp.concatenate(pieces, 0) * corr_scale


def correlate_back(grad_volume, winter_tile, matched):
    channels, height, tile_cols = winter_tile.shape
    disp_side = 2 * RADIUS + 1
    wide_cols = tile_cols + 2 * RADIUS
    corr_scale = 1.0 / math.sqrt(channels)
    grad_feat = jnp.zeros(winter_tile.shape, jnp.float32)
    grad_block = jnp.zeros(matched.shape, jnp.float32)
    for row_shift in range(disp_side):
        band_cut = grad_volume[row_shift * disp_side : (row_shift + 1) * disp_side].transpose(
            1, 2, 0
        )
        placed = jnp.pad(band_cut, ((0, 0), (0, 0), (0, tile_cols)))
        placed = placed.reshape(height, tile_cols * (wide_cols + 1))[
            :, : tile_cols * wide_cols
        ].reshape(height, tile_cols, wide_cols)
        strip_rows = matched[:, row_shift : row_shift + height, :]
        grad_feat = grad_feat + jnp.einsum(
            "ijm,cim->cij", placed, strip_rows, preferred_element_type=jnp.float32
        )
        grad_block = grad_block.at[:, row_shift : row_shift + height, :].add(
            jnp.einsum("ijm,cij->cim", placed, winter_tile, preferred_element_type=jnp.float32)
        )
    return (grad_feat * corr_scale, grad_block * corr_scale)


def body(winter, summer, offsets, feat_weight, bn_gain, bn_shift, w_first, w_second, cotangent):
    channels, tile_rows, tile_cols = winter.shape
    rim_width = RADIUS + 1
    row_count = lax.axis_size("row")
    col_count = lax.axis_size("col")
    row_at = lax.axis_index("row")
    col_at = lax.axis_index("col")
    height = tile_rows * row_count
    full_width = tile_cols * col_count
    pixel_count = float(height * full_width)

    def inside_mask(rim_cells):
        row_pos = (
            row_at * tile_rows - rim_cells + jnp.arange(tile_rows + 2 * rim_cells, dtype=jnp.int32)
        )
        col_pos = (
            col_at * tile_cols - rim_cells + jnp.arange(tile_cols + 2 * rim_cells, dtype=jnp.int32)
        )
        return ((row_pos >= 0) & (row_pos < height))[:, None] & (
            (col_pos >= 0) & (col_pos < full_width)
        )[None, :]

    def offset_at(component, row_pick, col_pick):
        return lax.dynamic_slice(offsets, (component, row_pick, col_pick), (1, 1, 1)).reshape(())

    my_row_step = offset_at(0, row_at, col_at)
    my_col_step = offset_at(1, row_at, col_at)
    winter_ext = extended(winter, (("row", 1), ("col", 2)), 1)
    winter_feat = conv_local(winter_ext, feat_weight).astype(jnp.bfloat16)
    summer_ext = extended(summer, (("row", 1), ("col", 2)), rim_width)
    summer_feat = jnp.where(
        inside_mask(RADIUS)[None], conv_local(summer_ext, feat_weight), 0.0
    ).astype(jnp.bfloat16)
    from_left = shifted(summer_feat, "col", 1)
    from_right = shifted(summer_feat, "col", -1)
    column_trio = jnp.stack([from_left, summer_feat, from_right])
    trio_above = shifted(column_trio, "row", 1)
    trio_below = shifted(column_trio, "row", -1)
    neighbour_grid = jnp.stack([trio_above, column_trio, trio_below])
    row_choice = lax.dynamic_index_in_dim(neighbour_grid, my_row_step + 1, 0, False)
    matched = lax.dynamic_index_in_dim(row_choice, my_col_step + 1, 0, False)
    cost_volume = correlate(winter_feat, matched)
    bn_sums = lax.psum(
        (jnp.sum(cost_volume, axis=(1, 2)), jnp.sum(cost_volume * cost_volume, axis=(1, 2))),
        ("row", "col"),
    )
    channel_mean = bn_sums[0] / pixel_count
    channel_var = bn_sums[1] / pixel_count - channel_mean * channel_mean
    inv_std = lax.rsqrt(channel_var + 1e-05)
    centred = (cost_volume - channel_mean[:, None, None]) * inv_std[:, None, None]
    pre_norm = bn_gain[:, None, None] * centred + bn_shift[:, None, None]
    normed = jax.nn.silu(pre_norm).astype(jnp.bfloat16)
    normed_ext = extended(normed, (("row", 1), ("col", 2)), 1)
    hidden_pre = conv_local(normed_ext, w_first)
    hidden = jax.nn.silu(hidden_pre).astype(jnp.bfloat16)
    hidden_ext = extended(hidden, (("row", 1), ("col", 2)), 1)
    refined = conv_local(hidden_ext, w_second).astype(jnp.bfloat16)
    cotangent_ext = extended(cotangent, (("row", 1), ("col", 2)), 1)
    grad_second = weight_term(cotangent, hidden_ext)
    grad_hidden = (
        conv_local(cotangent_ext, flip_weight(w_second, hidden.shape[0])) * silu_slope(hidden_pre)
    ).astype(jnp.bfloat16)
    hidden_grad_ext = extended(grad_hidden, (("row", 1), ("col", 2)), 1)
    grad_first = weight_term(grad_hidden, normed_ext)
    grad_normed = conv_local(hidden_grad_ext, flip_weight(w_first, normed.shape[0]))
    grad_pre = grad_normed * silu_slope(pre_norm)
    grad_sums = lax.psum(
        (jnp.sum(grad_pre, axis=(1, 2)), jnp.sum(grad_pre * centred, axis=(1, 2))), ("row", "col")
    )
    grad_volume = (
        bn_gain[:, None, None]
        * inv_std[:, None, None]
        * (
            grad_pre
            - grad_sums[0][:, None, None] / pixel_count
            - centred * grad_sums[1][:, None, None] / pixel_count
        )
    ).astype(jnp.bfloat16)
    grad_wfeat, grad_block = correlate_back(grad_volume, winter_feat, matched)
    grad_wfeat = grad_wfeat.astype(jnp.bfloat16)
    grad_block = grad_block.astype(jnp.bfloat16)
    zero_block = jnp.zeros_like(grad_block)
    from_above = shifted(jnp.where(my_row_step == 1, grad_block, zero_block), "row", 1)
    from_below = shifted(jnp.where(my_row_step == -1, grad_block, zero_block), "row", -1)
    own_block = jnp.where(my_row_step == 0, grad_block, zero_block)
    arrivals = [from_above, own_block, from_below]
    arrival_steps = [
        offset_at(1, jnp.clip(row_at - 1, 0, row_count - 1), col_at),
        my_col_step,
        offset_at(1, jnp.clip(row_at + 1, 0, row_count - 1), col_at),
    ]

    def collect(col_step):
        collected = jnp.zeros(grad_block.shape, jnp.float32)
        for arrival, step_value in zip(arrivals, arrival_steps):
            collected = collected + jnp.where(
                step_value == col_step, arrival.astype(jnp.float32), 0.0
            )
        return collected

    returned = collect(0)
    returned = returned + shifted(collect(1).astype(jnp.bfloat16), "col", 1).astype(jnp.float32)
    returned = returned + shifted(collect(-1).astype(jnp.bfloat16), "col", -1).astype(jnp.float32)
    wgrad_ext = extended(grad_wfeat, (("row", 1), ("col", 2)), 1)
    grad_winter = conv_local(wgrad_ext, flip_weight(feat_weight, channels)).astype(jnp.bfloat16)
    feat_term = weight_term(grad_wfeat, winter_ext)
    grad_sfeat = jnp.where(inside_mask(RADIUS)[None], returned, 0.0).astype(jnp.bfloat16)
    feat_term = feat_term + weight_term(grad_sfeat, summer_ext)
    grad_sext = conv_local(
        jnp.pad(grad_sfeat, ((0, 0), (2, 2), (2, 2))), flip_weight(feat_weight, channels)
    )
    right_strip = shifted(grad_sext[:, :, -rim_width:].astype(jnp.bfloat16), "col", 1).astype(
        jnp.float32
    )
    left_strip = shifted(grad_sext[:, :, :rim_width].astype(jnp.bfloat16), "col", -1).astype(
        jnp.float32
    )
    core_cols = grad_sext[:, :, rim_width : rim_width + tile_cols]
    core_cols = core_cols.at[:, :, :rim_width].add(right_strip)
    core_cols = core_cols.at[:, :, tile_cols - rim_width :].add(left_strip)
    lower_strip = shifted(core_cols[:, -rim_width:, :].astype(jnp.bfloat16), "row", 1).astype(
        jnp.float32
    )
    upper_strip = shifted(core_cols[:, :rim_width, :].astype(jnp.bfloat16), "row", -1).astype(
        jnp.float32
    )
    core_rows = core_cols[:, rim_width : rim_width + tile_rows, :]
    core_rows = core_rows.at[:, :rim_width, :].add(lower_strip)
    core_rows = core_rows.at[:, tile_rows - rim_width :, :].add(upper_strip)
    grad_summer = core_rows.astype(jnp.bfloat16)
    weight_sums = lax.psum((feat_term, grad_first, grad_second), ("row", "col"))
    return (
        refined,
        grad_winter,
        grad_summer,
        weight_sums[0],
        weight_sums[1],
        weight_sums[2],
        grad_sums[1],
        grad_sums[0],
    )


def solution(mesh):
    in_specs = (
        P(None, "row", "col"),
        P(None, "row", "col"),
        P(),
        P(),
        P(),
        P(),
        P(),
        P(),
        P(None, "row", "col"),
    )
    out_specs = (
        P(None, "row", "col"),
        P(None, "row", "col"),
        P(None, "row", "col"),
        P(),
        P(),
        P(),
        P(),
        P(),
    )
    return jax.shard_map(body, mesh=mesh, in_specs=in_specs, out_specs=out_specs, check_vma=False)
```

profile of v0, /device:TPU:1, one launch (start us, length us, event | category | flops | bytes accessed | tf_op | source)
XLA Modules:
  0.0 1178.7 jit_solution(884834388393214883)
XLA Ops:
  79.0 5.6 fusion.90
  85.8 7.5 collective-permute-start.10
  107.3 92.0 %collective-permute-done.1 = bf16[256,1,128]{2,0,1:T(8,128)(2,1)S(1)} collective-permute-done((bf16[256,1,128]{2,0,1:T(8,128)(2,1)S(1)}, bf16[256,1,128]{2,0,1:T(8,128)(2,1)S(1)}, u32[]{:S(2)}, u32[]{:S(2)}) %collective-permute-start.1) | collective-permute-done | bytes 65568 | tf_op jit(solution)/shard_map/ppermute | solution.py:19
  225.2 13.2 %copy.174 = bf16[2304,16,128]{0,2,1:T(8,128)(2,1)} copy(bf16[2304,16,128]{2,0,1:T(8,128)(2,1)} %fusion.67) | data formatting | bytes 18874368 | tf_op jit(solution)/shard_map/concatenate | solution.py:36
  238.5 6.5 convolution_convert_fusion.1
  284.2 5.3 reshape.706
  300.2 5.2 reshape.704
  316.0 5.2 reshape.702
  331.9 5.4 reshape.700
  348.1 5.2 reshape.698
  379.7 5.1 reshape.694
  405.6 9.0 concatenate.214
  414.8 67.4 %all-reduce.21 = (f32[81]{0:T(128)S(1)}, f32[81]{0:T(128)S(1)}) all-reduce(f32[81]{0:T(128)S(1)} %get-tuple-element.191, f32[81]{0:T(128)S(1)} %get-tuple-element.190), channel_id=1, replica_groups=mesh['row'=16,'col'=8] {'row','col'}, use_global_device_ids=true, to_apply=%region_3.4 | all-reduce | flops 162 | bytes 1296 | tf_op jit(solution)/shard_map/psum | solution.py:158
  511.0 14.8 %concatenate.248 = f32[81,2048]{1,0:T(8,128)} concatenate(f32[9,2048]{1,0:T(8,128)} %copy.334, f32[9,2048]{1,0:T(8,128)} %copy.336, f32[9,2048]{1,0:T(8,128)} %copy.338, f32[9,2048]{1,0:T(8,128)} %copy.340, f32[9,2048]{1,0:T(8,128)} %copy.342, f32[9,2048]{1,0:T(8,128)} %copy.344, f32[9,2048]{1,0:T(8,128)} %copy.346, f32[9,2048]{1,0:T(8,128)} %copy.348, f32[9,2048]{1,0:T(8,128)} %copy.350), dimensions={0} | concatenate | bytes 1327104 | tf_op jit(solution)/shard_map/concatenate | solution.py:88
  542.5 29.2 %concatenate.220 = bf16[729,16,128]{2,0,1:T(8,128)(2,1)} concatenate(bf16[81,16,128]{2,0,1:T(8,128)(2,1)} %get-tuple-element.276, bf16[81,16,128]{2,0,1:T(8,128)(2,1)} %get-tuple-element.245, bf16[81,16,128]{2,0,1:T(8,128)(2,1)} %get-tuple-element.225, bf16[81,16,128]{2,0,1:T(8,128)(2,1)} %get-tuple-element.277, bf16[81,16,128]{2,0,1:T(8,128)(2,1)} %copy-done.12, ...), dimensions={0} | concatenate | bytes 5971968 | tf_op jit(solution)/shard_map/concatenate | solution.py:36
  605.6 72.3 %all-reduce.20 = (f32[81]{0:T(128)S(1)}, f32[81]{0:T(128)S(1)}) all-reduce(f32[81]{0:T(128)S(1)} %get-tuple-element.189, f32[81]{0:T(128)S(1)} %get-tuple-element.188), channel_id=1, replica_groups=mesh['row'=16,'col'=8] {'row','col'}, use_global_device_ids=true, to_apply=%region_7.8 | all-reduce | flops 162 | bytes 1296 | tf_op jit(solution)/shard_map/psum | solution.py:182
  723.2 5.3 reshape.725
  865.4 22.0 %collective-permute-done.28 = bf16[256,1,128]{0,2,1:T(8,128)(2,1)S(1)} collective-permute-done((bf16[256,1,128]{0,2,1:T(8,128)(2,1)S(1)}, bf16[256,1,128]{0,2,1:T(8,128)(2,1)S(1)}, u32[]{:S(2)}, u32[]{:S(2)}) %collective-permute-start.28) | collective-permute-done | bytes 65568 | tf_op jit(solution)/shard_map/ppermute | solution.py:16
  918.9 5.8 collective-permute-done.34
  953.2 14.7 %reshape.741 = bf16[2304,3588]{0,1:T(8,128)(2,1)} reshape(bf16[2304,26,138]{0,2,1:T(8,128)(2,1)} %slice_dynamic-update-slice_fusion) | data formatting | bytes 33067008 | tf_op jit(solution)/shard_map/reshape | solution.py:43
  967.9 10.7 convolution_bitcast_fusion
  990.2 7.7 fusion
  1021.4 6.4 convolution_convert_fusion
  1044.6 122.2 %all-reduce.25.cloned.1.call-done = (f32[256,2304]{1,0:T(8,128)}, f32[64,729]{1,0:T(8,128)}, f32[32,576]{1,0:T(8,128)}) async-done(((f32[256,2304]{1,0:T(8,128)}, f32[64,729]{1,0:T(8,128)}, f32[32,576]{1,0:T(8,128)}), (f32[256,2304]{1,0:T(8,128)}, f32[64,729]{1,0:T(8,128)}, f32[32,576]{1,0:T(8,128)})) %all-reduce.25.cloned.1.call-update) | async-done | bytes 2619664 | tf_op jit(solution)/shard_map/psum | solution.py:246
  (503 shorter events, 608.4 us)
Async XLA Ops:
  7.2 1159.6 %all-reduce.25.cloned.1.call-start = ((), (), s32[]{:S(2)}) async-start(), calls=%async_computation | async-start | bytes 5275648 | tf_op jit(solution)/shard_map/psum | solution.py:246
  46.8 32.1 %collective-permute-start.8 = (bf16[256,24,136]{0,2,1:T(8,128)(2,1)}, bf16[256,24,136]{0,2,1:T(8,128)(2,1)}, u32[]{:S(2)}, u32[]{:S(2)}) collective-permute-start(bf16[256,24,136]{0,2,1:T(8,128)(2,1)} %select_convert_fusion.1), channel_id=1, source_target_pairs={{0,1},{1,2},{2,3},{3,4},{4,5},{5,6},{6,7},{8,9},{9,10},{10,11},{11... | collective-permute-start | bytes 5013512 | tf_op jit(solution)/shard_map/ppermute | solution.py:27
  48.7 30.2 %collective-permute-start.9 = (bf16[256,24,136]{0,2,1:T(8,128)(2,1)}, bf16[256,24,136]{0,2,1:T(8,128)(2,1)}, u32[]{:S(2)}, u32[]{:S(2)}) collective-permute-start(bf16[256,24,136]{0,2,1:T(8,128)(2,1)} %select_convert_fusion.1), channel_id=1, source_target_pairs={{1,0},{2,1},{3,2},{4,3},{5,4},{6,5},{7,6},{9,8},{10,9},{11,10},{12... | collective-permute-start | bytes 5013512 | tf_op jit(solution)/shard_map/ppermute | solution.py:27
  54.2 51.8 %collective-permute-start = (bf16[256,1,128]{2,0,1:T(8,128)(2,1)}, bf16[256,1,128]{2,0,1:T(8,128)(2,1)S(1)}, u32[]{:S(2)}, u32[]{:S(2)}) collective-permute-start(bf16[256,1,128]{2,0,1:T(8,128)(2,1)} %get-tuple-element.222), channel_id=1, source_target_pairs={{0,8},{8,16},{16,24},{24,32},{32,40},{40,48},{48,56},{56,64},{64,7... | collective-permute-start | bytes 196616 | tf_op jit(solution)/shard_map/ppermute | solution.py:16
  57.6 19.3 %collective-permute-start.20 = (bf16[32,1,128]{2,1,0:T(2,128)(2,1)S(1)}, bf16[32,1,128]{2,1,0:T(2,128)(2,1)S(1)}, u32[]{:S(2)}, u32[]{:S(2)}) collective-permute-start(bf16[32,1,128]{2,1,0:T(2,128)(2,1)S(1)} %get-tuple-element.264), channel_id=1, source_target_pairs={{0,8},{8,16},{16,24},{24,32},{32,40},{40,48},{48,56},{56,64},{64,7... | collective-permute-start | bytes 24584 | tf_op jit(solution)/shard_map/ppermute | solution.py:16
  60.9 16.1 %collective-permute-start.21 = (bf16[32,1,128]{2,1,0:T(2,128)(2,1)S(1)}, bf16[32,1,128]{2,1,0:T(2,128)(2,1)S(1)}, u32[]{:S(2)}, u32[]{:S(2)}) collective-permute-start(bf16[32,1,128]{2,1,0:T(2,128)(2,1)S(1)} %get-tuple-element.265), channel_id=1, source_target_pairs={{8,0},{16,8},{24,16},{32,24},{40,32},{48,40},{56,48},{64,56},{72,6... | collective-permute-start | bytes 24584 | tf_op jit(solution)/shard_map/ppermute | solution.py:19
  84.5 160.4 %collective-permute-start.11 = (bf16[3,256,24,136]{1,3,2,0:T(8,128)(2,1)}, bf16[3,256,24,136]{1,3,2,0:T(8,128)(2,1)}, u32[]{:S(2)}, u32[]{:S(2)}) collective-permute-start(bf16[3,256,24,136]{1,3,2,0:T(8,128)(2,1)} %get-tuple-element.204), channel_id=1, source_target_pairs={{8,0},{16,8},{24,16},{32,24},{40,32},{48,40},{56,48},{64,56},{72,6... | collective-permute-start | bytes 15040520 | tf_op jit(solution)/shard_map/ppermute | solution.py:27
  85.8 159.2 %collective-permute-start.10 = (bf16[3,256,24,136]{1,3,2,0:T(8,128)(2,1)}, bf16[3,256,24,136]{1,3,2,0:T(8,128)(2,1)}, u32[]{:S(2)}, u32[]{:S(2)}) collective-permute-start(bf16[3,256,24,136]{1,3,2,0:T(8,128)(2,1)} %get-tuple-element.204), channel_id=1, source_target_pairs={{0,8},{8,16},{16,24},{24,32},{32,40},{40,48},{48,56},{56,64},{64,7... | collective-permute-start | bytes 15040520 | tf_op jit(solution)/shard_map/ppermute | solution.py:27
  102.1 97.2 %collective-permute-start.1 = (bf16[256,1,128]{2,0,1:T(8,128)(2,1)S(1)}, bf16[256,1,128]{2,0,1:T(8,128)(2,1)S(1)}, u32[]{:S(2)}, u32[]{:S(2)}) collective-permute-start(bf16[256,1,128]{2,0,1:T(8,128)(2,1)S(1)} %get-tuple-element.221), channel_id=1, source_target_pairs={{8,0},{16,8},{24,16},{32,24},{40,32},{48,40},{56,48},{64,56},{72,6... | collective-permute-start | bytes 196616 | tf_op jit(solution)/shard_map/ppermute | solution.py:19
  485.0 40.9 %collective-permute-start.12 = (bf16[81,1,128]{2,0,1:T(8,128)(2,1)}, bf16[81,1,128]{2,0,1:T(8,128)(2,1)S(1)}, u32[]{:S(2)}, u32[]{:S(2)}) collective-permute-start(bf16[81,1,128]{2,0,1:T(8,128)(2,1)} %get-tuple-element.246), channel_id=1, source_target_pairs={{0,8},{8,16},{16,24},{24,32},{32,40},{40,48},{48,56},{56,64},{64,7... | collective-permute-start | bytes 62216 | tf_op jit(solution)/shard_map/ppermute | solution.py:16
  487.4 38.5 %collective-permute-start.13 = (bf16[81,1,128]{2,0,1:T(8,128)(2,1)}, bf16[81,1,128]{2,0,1:T(8,128)(2,1)}, u32[]{:S(2)}, u32[]{:S(2)}) collective-permute-start(bf16[81,1,128]{2,0,1:T(8,128)(2,1)} %get-tuple-element.247), channel_id=1, source_target_pairs={{8,0},{16,8},{24,16},{32,24},{40,32},{48,40},{56,48},{64,56},{72,6... | collective-permute-start | bytes 62216 | tf_op jit(solution)/shard_map/ppermute | solution.py:19
  580.0 10.9 collective-permute-start.24
  591.1 11.1 collective-permute-start.26
  596.6 255.5 %collective-permute-start.18 = (bf16[64,18,1]{2,0,1:T(8,128)(2,1)}, bf16[64,18,1]{2,0,1:T(8,128)(2,1)}, u32[]{:S(2)}, u32[]{:S(2)}) collective-permute-start(bf16[64,18,1]{2,0,1:T(8,128)(2,1)} %get-tuple-element.255), channel_id=1, source_target_pairs={{0,1},{1,2},{2,3},{3,4},{4,5},{5,6},{6,7},{8,9},{9,10},{10,11},{11... | collective-permute-start | bytes 6920 | tf_op jit(solution)/shard_map/ppermute | solution.py:16
  600.2 251.9 %collective-permute-start.19 = (bf16[64,18,1]{2,0,1:T(8,128)(2,1)}, bf16[64,18,1]{2,0,1:T(8,128)(2,1)}, u32[]{:S(2)}, u32[]{:S(2)}) collective-permute-start(bf16[64,18,1]{2,0,1:T(8,128)(2,1)} %get-tuple-element.254), channel_id=1, source_target_pairs={{1,0},{2,1},{3,2},{4,3},{5,4},{6,5},{7,6},{9,8},{10,9},{11,10},{12... | collective-permute-start | bytes 6920 | tf_op jit(solution)/shard_map/ppermute | solution.py:19
  848.4 53.5 %collective-permute-start.32 = (bf16[256,24,136]{0,2,1:T(8,128)(2,1)S(1)}, bf16[256,24,136]{0,2,1:T(8,128)(2,1)S(1)}, u32[]{:S(2)}, u32[]{:S(2)}) collective-permute-start(bf16[256,24,136]{0,2,1:T(8,128)(2,1)S(1)} %broadcast_select_fusion.2), channel_id=1, source_target_pairs={{0,8},{8,16},{16,24},{24,32},{32,40},{40,48},{48,56},{56,64},{64,7... | collective-permute-start | bytes 5013512 | tf_op jit(solution)/shard_map/ppermute | solution.py:27
  850.8 51.1 %collective-permute-start.33 = (bf16[256,24,136]{0,2,1:T(8,128)(2,1)S(1)}, bf16[256,24,136]{0,2,1:T(8,128)(2,1)S(1)}, u32[]{:S(2)}, u32[]{:S(2)}) collective-permute-start(bf16[256,24,136]{0,2,1:T(8,128)(2,1)S(1)} %get-tuple-element.199), channel_id=1, source_target_pairs={{8,0},{16,8},{24,16},{32,24},{40,32},{48,40},{56,48},{64,56},{72,6... | collective-permute-start | bytes 5013512 | tf_op jit(solution)/shard_map/ppermute | solution.py:27
  859.3 28.1 %collective-permute-start.28 = (bf16[256,1,128]{0,2,1:T(8,128)(2,1)S(1)}, bf16[256,1,128]{0,2,1:T(8,128)(2,1)S(1)}, u32[]{:S(2)}, u32[]{:S(2)}) collective-permute-start(bf16[256,1,128]{0,2,1:T(8,128)(2,1)S(1)} %get-tuple-element.217), channel_id=1, source_target_pairs={{0,8},{8,16},{16,24},{24,32},{32,40},{40,48},{48,56},{56,64},{64,7... | collective-permute-start | bytes 196616 | tf_op jit(solution)/shard_map/ppermute | solution.py:16
  863.3 28.0 %collective-permute-start.29 = (bf16[256,1,128]{0,2,1:T(8,128)(2,1)S(1)}, bf16[256,1,128]{0,2,1:T(8,128)(2,1)S(1)}, u32[]{:S(2)}, u32[]{:S(2)}) collective-permute-start(bf16[256,1,128]{0,2,1:T(8,128)(2,1)S(1)} %get-tuple-element.218), channel_id=1, source_target_pairs={{8,0},{16,8},{24,16},{32,24},{40,32},{48,40},{56,48},{64,56},{72,6... | collective-permute-start | bytes 196616 | tf_op jit(solution)/shard_map/ppermute | solution.py:19
  903.6 21.0 %collective-permute-start.34 = (bf16[256,24,136]{0,2,1:T(8,128)(2,1)S(1)}, bf16[256,24,136]{0,2,1:T(8,128)(2,1)S(1)}, u32[]{:S(2)}, u32[]{:S(2)}) collective-permute-start(bf16[256,24,136]{0,2,1:T(8,128)(2,1)S(1)} %get-tuple-element.201), channel_id=1, source_target_pairs={{0,1},{1,2},{2,3},{3,4},{4,5},{5,6},{6,7},{8,9},{9,10},{10,11},{11... | collective-permute-start | bytes 5013512 | tf_op jit(solution)/shard_map/ppermute | solution.py:27
  906.3 23.1 %collective-permute-start.35 = (bf16[256,24,136]{0,2,1:T(8,128)(2,1)S(1)}, bf16[256,24,136]{0,2,1:T(8,128)(2,1)S(1)}, u32[]{:S(2)}, u32[]{:S(2)}) collective-permute-start(bf16[256,24,136]{0,2,1:T(8,128)(2,1)S(1)} %get-tuple-element.202), channel_id=1, source_target_pairs={{1,0},{2,1},{3,2},{4,3},{5,4},{6,5},{7,6},{9,8},{10,9},{11,10},{12... | collective-permute-start | bytes 5013512 | tf_op jit(solution)/shard_map/ppermute | solution.py:27
  988.3 20.5 %collective-permute-start.36 = (bf16[256,26,5]{0,1,2:T(8,128)(2,1)}, bf16[256,26,5]{0,1,2:T(8,128)(2,1)}, u32[]{:S(2)}, u32[]{:S(2)}) collective-permute-start(bf16[256,26,5]{0,1,2:T(8,128)(2,1)} %get-tuple-element.206), channel_id=1, source_target_pairs={{0,1},{1,2},{2,3},{3,4},{4,5},{5,6},{6,7},{8,9},{9,10},{10,11},{11... | collective-permute-start | bytes 199688 | tf_op jit(solution)/shard_map/ppermute | solution.py:27
  1016.6 15.6 %collective-permute-start.38 = (bf16[256,5,128]{0,1,2:T(8,128)(2,1)S(1)}, bf16[256,5,128]{0,1,2:T(8,128)(2,1)}, u32[]{:S(2)}, u32[]{:S(2)}) collective-permute-start(bf16[256,5,128]{0,1,2:T(8,128)(2,1)S(1)} %get-tuple-element.208), channel_id=1, source_target_pairs={{0,8},{8,16},{16,24},{24,32},{32,40},{40,48},{48,56},{56,64},{64,7... | collective-permute-start | bytes 983048 | tf_op jit(solution)/shard_map/ppermute | solution.py:27
  1020.1 17.6 %collective-permute-start.39 = (bf16[256,5,128]{0,1,2:T(8,128)(2,1)}, bf16[256,5,128]{0,1,2:T(8,128)(2,1)}, u32[]{:S(2)}, u32[]{:S(2)}) collective-permute-start(bf16[256,5,128]{0,1,2:T(8,128)(2,1)} %get-tuple-element.207), channel_id=1, source_target_pairs={{8,0},{16,8},{24,16},{32,24},{40,32},{48,40},{56,48},{64,56},{72,6... | collective-permute-start | bytes 983048 | tf_op jit(solution)/shard_map/ppermute | solution.py:27
  (89 other events, 1868.1 us)
Sparse Core Ops, SparseCore 0:
  1008.9 157.7 all-reduce.24
where the time goes:
time: 1200 us; the launch traced here: 1180 us
  local copies, waits for them, and re-layouts  469 us (39%)
  waiting for transfers between devices  272 us (23%)
  blocking collectives  140 us (12%)
  matrix products  114 us (10%)
  starting transfers between devices  105 us (9%)
  other arithmetic  52.3 us (4%)
  between operations  26.7 us (2%)
    psum x1, waiting for transfers between devices, body(): weight_sums = lax.psum((feat_term, grad_first, grad_second), ('row', 'col'))  122 us
    ppermute x14, waiting for transfers between devices, extended(): lax.ppermute(lax.slice_in_dim(block, 0, width, axis=dim), axis, backward)  110 us
    unnamed x217, local copies, waits for them, and re-layouts  87.8 us
    psum x1, blocking collectives, body(): lax.psum((jnp.sum(grad_pre, axis=(1, 2)), jnp.sum(grad_pre * centred, axi...  72.3 us
    psum x1, blocking collectives, body(): lax.psum((jnp.sum(cost_volume, axis=(1, 2)), jnp.sum(cost_volume * cost_v...  67.4 us
    concatenate x9, local copies, waits for them, and re-layouts, patches(): jnp.concatenate([padded[:, shift_row:shift_row + height, shift_col:shift_...  51.2 us
    ppermute x14, starting transfers between devices, extended(): lax.ppermute(lax.slice_in_dim(block, block.shape[dim] - width, None, axis...  48.5 us
    reshape x9, local copies, waits for them, and re-layouts, correlate(): flattened.reshape(height, tile_cols, wide_cols + 1)[:, :, :disp_side]  46.6 us
  transfers between devices with their start and end apart: 41, of which 15 were waited for; matrix products, arithmetic and copies ran while one was open for 29% of the time, Pallas kernels for 0%

commit v1 on v0

v1 whole, which is shorter than its diff:
```python
import functools

import jax
import jax.numpy as jnp
from jax import lax
from jax.experimental import pallas as pl
from jax.experimental.pallas import tpu as pltpu
from jax.sharding import PartitionSpec as P

MESH = pl.DeviceIdType.MESH
C = 256
TR = 16
TC = 128
CH = 144
NROW = 16
NCOL = 8
PIXELS = 262144.0
F32 = jnp.float32
BF16 = jnp.bfloat16
VMEM_LIMIT = 58 * 1024 * 1024
AROUND = [(a, b) for a in (-1, 0, 1) for b in (-1, 0, 1) if (a, b) != (0, 0)]
NT = (((1,), (1,)), ((), ()))


def vspec():
    return pl.BlockSpec(memory_space=pltpu.VMEM)


def anyspec():
    return pl.BlockSpec(memory_space=pl.ANY)


def sspec():
    return pl.BlockSpec(memory_space=pltpu.SMEM)


def sds(shape, dtype):
    return jax.ShapeDtypeStruct(shape, dtype)


def call(kernel, outs, ins, scratch=(), in_specs=None, out_specs=None, **params):
    results = pl.pallas_call(
        kernel,
        out_shape=outs,
        in_specs=in_specs or [vspec() for _ in ins],
        out_specs=out_specs or [vspec() for _ in outs],
        scratch_shapes=list(scratch),
        compiler_params=pltpu.CompilerParams(vmem_limit_bytes=VMEM_LIMIT, **params),
    )(*ins)
    return list(results)


def rl(value, shift, axis):
    shift %= value.shape[axis]
    return value if shift == 0 else pltpu.roll(value, shift, axis)


def lane_of(shape):
    return lax.broadcasted_iota(jnp.int32, shape, 1)


def dot(a, b):
    return jnp.dot(a, b, preferred_element_type=F32)


def dot_nt(a, b):
    return lax.dot_general(a, b, NT, preferred_element_type=F32)


def pack_cols(row, cols, count=TR):
    total = None
    for y in range(count):
        value = row(y)
        lane = lane_of(value.shape)
        if total is None:
            total = jnp.zeros(value.shape, F32)
        for col, base in cols:
            total = jnp.where(lane == base + y, rl(value, base + y - col, 1), total)
    return total


ONE = [(0, 0), (127, 64)]
TWO = [(0, 0), (1, 16), (126, 64), (127, 80)]


def device_at(drow, dcol):
    row = lax.rem(lax.axis_index("row") + drow + NROW, NROW)
    col = lax.rem(lax.axis_index("col") + dcol + NCOL, NCOL)
    return (row, col)


def greet(steps):
    both = sorted(set(steps) | {(-a, -b) for a, b in steps})
    barrier = pltpu.get_barrier_semaphore()
    for step in both:
        pl.semaphore_signal(barrier, inc=1, device_id=device_at(*step), device_id_type=MESH)
    pl.semaphore_wait(barrier, len(both))


def exchange_kernel(moves, n_in, *refs):
    ins = refs[:n_in]
    outs = refs[n_in : n_in + len(moves)]
    send, recv = refs[n_in + len(moves) :]
    greet([m[3] for m in moves])
    copies = []
    for k, (which, start, size, step) in enumerate(moves):
        copies.append(
            pltpu.make_async_remote_copy(
                src_ref=ins[which].at[pl.ds(start, size)],
                dst_ref=outs[k],
                send_sem=send.at[k],
                recv_sem=recv.at[k],
                device_id=device_at(*step),
                device_id_type=MESH,
            )
        )
    for copy in copies:
        copy.start()
    for copy in copies:
        copy.wait()


def exchange(arrays, moves, collective_id):
    outs = [sds((size,) + arrays[which].shape[1:], arrays[which].dtype) for which, _, size, _ in moves]
    return call(
        functools.partial(exchange_kernel, moves, len(arrays)),
        outs,
        arrays,
        [pltpu.SemaphoreType.DMA((len(moves),)), pltpu.SemaphoreType.DMA((len(moves),))],
        in_specs=[anyspec() for _ in arrays],
        out_specs=[anyspec() for _ in moves],
        collective_id=collective_id,
        has_side_effects=True,
    )


def load_rows(x_ref, wide):
    wide[...] = x_ref[...].astype(F32)


def strided(wide, y, channels):
    return wide[pl.ds(y, channels, stride=TR), :]


def edges_kernel(w_ref, s_ref, c_ref, rows_out, pack_out, crows_out, cpack_out, wide, cwide):
    for k, ref in enumerate((w_ref, s_ref)):
        wide[...] = ref[...].astype(F32)
        rows_out[k] = strided(wide, 0, C).astype(BF16)
        rows_out[2 + k] = strided(wide, TR - 1, C).astype(BF16)
        pack_out[k] = pack_cols(lambda y: strided(wide, y, C), ONE).astype(BF16)
    cwide[...] = c_ref[...].astype(F32)
    for k, y in enumerate((0, 1, 14, 15)):
        crows_out[k] = strided(cwide, y, 32).astype(BF16)
    cpack_out[0] = pack_cols(lambda y: strided(cwide, y, 32), TWO).astype(BF16)


def edges2_kernel(w_ref, s_ref, rows_out, pack_out):
    for k, ref in enumerate((w_ref, s_ref)):
        rows_out[k] = ref[:, 0:TC]
        rows_out[2 + k] = ref[:, (TR - 1) * TC : TR * TC]
        pack_out[k] = pack_cols(
            lambda y: ref[:, y * TC : (y + 1) * TC].astype(F32), ONE
        ).astype(BF16)


def halo_moves(base):
    return [(0, 2, 2, (1, 0)), (0, 0, 2, (-1, 0))] + [(1, 0, 2, step) for step in AROUND if step[1] != 0]


SIDE_STEPS = [step for step in AROUND if step[1] != 0]


def halo_cols(packs, k):
    first_row = lax.axis_index("row") == 0
    last_row = lax.axis_index("row") == NROW - 1
    first_col = lax.axis_index("col") == 0
    last_col = lax.axis_index("col") == NCOL - 1
    get = lambda a, b: packs[(a, b)][k].astype(F32)
    total = jnp.zeros((C, TC), F32)
    lane = lane_of((C, TC))
    for side, source_base, dest, gone in ((-1, 64, 0, first_col), (1, 0, 64, last_col)):
        keep = jnp.logical_not(gone)
        up = keep & jnp.logical_not(first_row)
        down = keep & jnp.logical_not(last_row)
        mid = (lane >= dest + 1) & (lane < dest + 17) & keep
        total = jnp.where(mid, rl(get(0, side), dest + 1 - source_base, 1), total)
        total = jnp.where((lane == dest) & up, rl(get(-1, side), dest - source_base - 15, 1), total)
        total = jnp.where((lane == dest + 17) & down, rl(get(1, side), dest + 17 - source_base, 1), total)
    return total


def build_x3(x3, row, halo, count, channels, first_lane=0):
    for k in range(count):
        value = row(k)
        lane = lane_of(value.shape)
        at = slice(k * TC, (k + 1) * TC)
        left = jnp.where(lane == 0, rl(halo, -(first_lane + k), 1), rl(value, 1, 1))
        right = jnp.where(lane == TC - 1, rl(halo, TC - 1 - (64 + first_lane + k), 1), rl(value, -1, 1))
        x3[0:channels, at] = left.astype(BF16)
        x3[channels : 2 * channels, at] = value.astype(BF16)
        x3[2 * channels : 3 * channels, at] = right.astype(BF16)


def end_row(ref, gone):
    return jnp.where(gone, 0.0, ref.astype(F32))


def conv_chunk(w_ref, x3, start, width):
    total = None
    depth = x3.shape[0]
    for a in range(3):
        term = dot(w_ref[:, a * depth : (a + 1) * depth], x3[:, start + a * TC : start + a * TC + width])
        total = term if total is None else total + term
    return total


PACK_PLACES = [(-a, -b) for a, b in SIDE_STEPS]


def feat_kernel(k, summer, x_ref, top, bottom, p0, p1, p2, p3, p4, p5, w_ref, *rest):
    if summer:
        f_out, x3_out, wide = rest
    else:
        f_out, x3_out, wide = rest
    packs = dict(zip(PACK_PLACES, (p0, p1, p2, p3, p4, p5)))
    wide[...] = x_ref[...].astype(F32)
    first_row = lax.axis_index("row") == 0
    last_row = lax.axis_index("row") == NROW - 1

    def row(j):
        if j == 0:
            return end_row(top[k], first_row)
        if j == TR + 1:
            return end_row(bottom[k], last_row)
        return strided(wide, j - 1, C)

    build_x3(x3_out, row, halo_cols(packs, k), TR + 2, C)
    for n in range(4):
        value = conv_chunk(w_ref, x3_out, n * 512, 512)
        if summer:
            for j in range(4):
                wide[(n * 4 + j) * C : (n * 4 + j + 1) * C, :] = value[:, j * TC : (j + 1) * TC]
                f_out[n * 4 + j] = value[:, j * TC : (j + 1) * TC].astype(BF16)
        else:
            f_out[:, n * 512 : (n + 1) * 512] = value.astype(BF16)
    if summer:
        lane = lane_of((C, TC))
        total = jnp.zeros((C, TC), F32)
        for y in range(TR):
            value = wide[y * C : (y + 1) * C, :]
            low = (lane >= y * 8) & (lane < y * 8 + 4)
            high = (lane >= y * 8 + 4) & (lane < y * 8 + 8)
            total = jnp.where(low, rl(value, y * 8, 1), total)
            total = jnp.where(high, rl(value, y * 8 + 4 - 124, 1), total)
        f_out[TR] = total.astype(BF16)


def offset_of(off, part, row, col):
    return off[part * NROW * NCOL + row * NCOL + col]


def match_kernel(off, fp, out, strip, pstrip, send_buf, trio, ptrio, psend, lsem, sems, rsems):
    row = lax.axis_index("row")
    col = lax.axis_index("col")
    steps = [(1, 0), (-1, 0), (2, 0), (-2, 0), (0, 1), (0, -1), (0, 2), (0, -2)]
    own = [
        pltpu.make_async_copy(fp.at[pl.ds(0, TR)], strip.at[pl.ds(20, TR)], lsem.at[0]),
        pltpu.make_async_copy(fp.at[pl.ds(TR, 1)], pstrip.at[pl.ds(2, 1)], lsem.at[1]),
    ]
    for copy in own:
        copy.start()
    greet(steps)

    def remote(k, src, dst, step):
        return pltpu.make_async_remote_copy(
            src_ref=src,
            dst_ref=dst,
            send_sem=sems.at[k],
            recv_sem=rsems.at[k],
            device_id=device_at(*step),
            device_id_type=MESH,
        )

    stage = [
        remote(0, fp.at[pl.ds(0, TR)], strip.at[pl.ds(4, TR)], (1, 0)),
        remote(1, fp.at[pl.ds(0, TR)], strip.at[pl.ds(36, TR)], (-1, 0)),
        remote(2, fp.at[pl.ds(12, 4)], strip.at[pl.ds(0, 4)], (2, 0)),
        remote(3, fp.at[pl.ds(0, 4)], strip.at[pl.ds(52, 4)], (-2, 0)),
        remote(4, fp.at[pl.ds(TR, 1)], pstrip.at[pl.ds(1, 1)], (1, 0)),
        remote(5, fp.at[pl.ds(TR, 1)], pstrip.at[pl.ds(3, 1)], (-1, 0)),
        remote(6, fp.at[pl.ds(TR, 1)], pstrip.at[pl.ds(0, 1)], (2, 0)),
        remote(7, fp.at[pl.ds(TR, 1)], pstrip.at[pl.ds(4, 1)], (-2, 0)),
    ]
    for copy in stage:
        copy.start()
    for copy in own:
        copy.wait()
    for copy in stage:
        copy.wait()

    def pick_of(dcol):
        return offset_of(off, 0, row, lax.rem(col + dcol + NCOL, NCOL)) + 1

    second = []
    for k, dcol in enumerate((-1, 1)):
        pick = pick_of(dcol)

        def fill(j, carry, k=k, pick=pick):
            send_buf[k, j] = strip[16 * pick + j]
            return carry

        lax.fori_loop(0, 24, fill, 0)
        copy = remote(8 + k, send_buf.at[k], trio.at[1 - dcol], (0, dcol))
        copy.start()
        second.append(copy)
    for k, dcol in enumerate((-2, -1, 1, 2)):
        pick = pick_of(dcol)
        for j in range(3):
            psend[k, j] = pstrip[pick + j]
        copy = remote(10 + k, psend.at[k], ptrio.at[2 - dcol], (0, dcol))
        copy.start()
        second.append(copy)
    pick = pick_of(0)

    def fill(j, carry):
        trio[1, j] = strip[16 * pick + j]
        return carry

    lax.fori_loop(0, 24, fill, 0)
    for j in range(3):
        ptrio[2, j] = pstrip[pick + j]
    for copy in second:
        copy.wait()
    my_row = row + offset_of(off, 0, row, col)
    my_col = col + offset_of(off, 1, row, col)
    dcol = my_col - col + 1
    zero = jnp.zeros((C, TC), BF16)
    for j in range(24):
        value = trio[dcol, j]
        if j < 4:
            value = jnp.where(my_row == 0, zero, value)
        if j >= 20:
            value = jnp.where(my_row == NROW - 1, zero, value)
        out[:, j * TC : (j + 1) * TC] = value
    low = lax.rem(lane_of((C, TC)), 8) < 4
    for j in range(3):
        right = jnp.where(my_col == NCOL - 1, zero, ptrio[dcol + 2, j]).astype(F32)
        left = jnp.where(my_col == 0, zero, ptrio[dcol, j]).astype(F32)
        value = jnp.where(low, right, left)
        if j == 0:
            value = jnp.where(my_row == 0, 0.0, value)
        if j == 2:
            value = jnp.where(my_row == NROW - 1, 0.0, value)
        out[:, (24 + j) * TC : (25 + j) * TC] = value.astype(BF16)


def match(offsets, fp):
    return call(
        match_kernel,
        [sds((C, 27 * TC), BF16)],
        [offsets, fp],
        [
            pltpu.VMEM((56, C, TC), BF16),
            pltpu.VMEM((5, C, TC), BF16),
            pltpu.VMEM((2, 24, C, TC), BF16),
            pltpu.VMEM((3, 24, C, TC), BF16),
            pltpu.VMEM((5, 3, C, TC), BF16),
            pltpu.VMEM((4, 3, C, TC), BF16),
            pltpu.SemaphoreType.DMA((2,)),
            pltpu.SemaphoreType.DMA((14,)),
            pltpu.SemaphoreType.DMA((14,)),
        ],
        in_specs=[sspec(), vspec()],
        collective_id=1,
        has_side_effects=True,
    )[0]


def bit_off(lane, bit):
    return (lane & bit) == 0


def shear(main, rim):
    low = lane_of((80, TC)) < 64
    w = jnp.where(low, jnp.concatenate([rim, main[0:72]], 0), jnp.concatenate([main[56:128], rim], 0))
    w = jnp.where(bit_off(lane_of((48, TC)), 32), w[0:48], w[32:80])
    w = jnp.where(bit_off(lane_of((32, TC)), 16), w[0:32], w[16:48])
    w = jnp.where(bit_off(lane_of((24, TC)), 8), w[0:24], w[8:32])
    lane = lane_of((16, TC))
    w = jnp.where(bit_off(lane, 4), rl(w, -4, 0)[0:16], w[8:24])
    w = jnp.where(bit_off(lane, 2), w, rl(w, -2, 0))
    w = jnp.where(bit_off(lane, 1), w, rl(w, -1, 0))
    return jnp.where(lax.broadcasted_iota(jnp.int32, (16, TC), 0) < 9, w, 0.0)


def unshear(value):
    lane = lane_of((16, TC))
    w = jnp.where(bit_off(lane, 1), value, rl(value, 1, 0))
    w = jnp.where(bit_off(lane, 2), w, rl(w, 2, 0))
    zeros = lambda n: jnp.zeros((n, TC), F32)
    padded = jnp.concatenate([w, zeros(8)], 0)
    w = jnp.where(bit_off(lane_of((24, TC)), 4), rl(padded, 4, 0), jnp.concatenate([zeros(8), w], 0))
    for n, bit in ((24, 8), (32, 16), (48, 32)):
        w = jnp.where(
            bit_off(lane_of((n + bit, TC)), bit),
            jnp.concatenate([w, zeros(bit)], 0),
            jnp.concatenate([zeros(bit), w], 0),
        )
    low = lambda n: lane_of((n, TC)) < 64
    main = jnp.concatenate(
        [
            jnp.where(low(56), w[8:64], 0.0),
            jnp.where(low(16), w[64:80], w[0:16]),
            jnp.where(low(56), 0.0, w[16:72]),
        ],
        0,
    )
    return main, jnp.where(low(8), w[0:8], w[72:80])


def row_sums(first, second):
    ones = jnp.ones((8, TC), F32)
    a = lax.dot_general(ones, first, NT, precision=lax.Precision.HIGHEST, preferred_element_type=F32)
    b = lax.dot_general(ones, second, NT, precision=lax.Precision.HIGHEST, preferred_element_type=F32)
    return jnp.where(lax.broadcasted_iota(jnp.int32, a.shape, 0) == 0, a, b)


def correlate_kernel(fw, m, cv, pack, sums, mt, rt, grim, s1, s2):
    for r in range(24):
        mt[r * TC : (r + 1) * TC, :] = m[:, r * TC : (r + 1) * TC].T
    for q in range(3):
        rt[q * TC : (q + 1) * TC, :] = m[:, (24 + q) * TC : (25 + q) * TC].T
    for n in range(4):
        grim[:, n * 512 : (n + 1) * 512] = dot(rt[...], fw[:, n * 512 : (n + 1) * 512])
    s1[...] = jnp.zeros_like(s1)
    s2[...] = jnp.zeros_like(s2)

    def at_row(y, carry):
        lanes = pl.ds(pl.multiple_of(y * TC, TC), TC)
        feat = fw[:, lanes]
        for a in range(9):
            main = dot(mt[pl.ds(pl.multiple_of((y + a) * TC, TC), TC), :], feat)
            rim = grim[pl.ds(pl.multiple_of((y + a + 12) * 8, 8), 8), lanes]
            value = shear(main, rim) * 0.0625
            rows = slice(a * 16, (a + 1) * 16)
            cv[y, rows, :] = value
            s1[rows, :] += value
            s2[rows, :] += value * value
        return carry

    lax.fori_loop(0, TR, at_row, 0)
    pack[0] = pack_cols(lambda y: cv[y], TWO)
    sums[...] = jnp.zeros_like(sums)
    sums[:, 0:CH] = row_sums(s1[...], s2[...])


def reduce_phases(value_ref, gather_col, gather_row, out, csend, crecv, rsend, rrecv, base=0):
    for count, axis, src, dst, send, recv in (
        (NCOL, "col", value_ref, gather_col, csend, crecv),
        (NROW, "row", out, gather_row, rsend, rrecv),
    ):
        copies = []
        for d in range(1, count):
            step = (0, d) if axis == "col" else (d, 0)
            copies.append(
                pltpu.make_async_remote_copy(
                    src_ref=src,
                    dst_ref=dst.at[d],
                    send_sem=send.at[d],
                    recv_sem=recv.at[d],
                    device_id=device_at(*step),
                    device_id_type=MESH,
                )
            )
        for copy in copies:
            copy.start()
        for copy in copies:
            copy.wait()
        dst[0] = src[...]
        me = lax.axis_index(axis)
        total = None
        for d in range(count):
            value = dst[lax.rem(me - d + count, count)]
            total = value if total is None else total + value
        out[...] = total


RING = [(0, d) for d in range(1, NCOL)] + [(d, 0) for d in range(1, NROW)]


def stats_kernel(moves, n_in, *refs):
    value = refs[0]
    ins = refs[1 : 1 + n_in]
    out = refs[1 + n_in]
    outs = refs[2 + n_in : 2 + n_in + len(moves)]
    gcol, grow, csend, crecv, rsend, rrecv, send, recv = refs[2 + n_in + len(moves) :]
    greet(RING + [m[3] for m in moves])
    copies = [
        pltpu.make_async_remote_copy(
            src_ref=ins[which].at[pl.ds(start, size)],
            dst_ref=outs[k],
            send_sem=send.at[k],
            recv_sem=recv.at[k],
            device_id=device_at(*step),
            device_id_type=MESH,
        )
        for k, (which, start, size, step) in enumerate(moves)
    ]
    for copy in copies:
        copy.start()
    reduce_phases(value, gcol, grow, out, csend, crecv, rsend, rrecv)
    for copy in copies:
        copy.wait()


def stats(value, arrays, moves, collective_id):
    outs = [sds(value.shape, F32)] + [
        sds((size,) + arrays[which].shape[1:], arrays[which].dtype) for which, _, size, _ in moves
    ]
    dma = pltpu.SemaphoreType.DMA
    return call(
        functools.partial(stats_kernel, moves, len(arrays)),
        outs,
        [value] + arrays,
        [
            pltpu.VMEM((NCOL,) + value.shape, F32),
            pltpu.VMEM((NROW,) + value.shape, F32),
            dma((NCOL,)),
            dma((NCOL,)),
            dma((NROW,)),
            dma((NROW,)),
            dma((max(1, len(moves)),)),
            dma((max(1, len(moves)),)),
        ],
        in_specs=[vspec()] + [anyspec() for _ in arrays],
        out_specs=[vspec()] + [anyspec() for _ in moves],
        collective_id=collective_id,
        has_side_effects=True,
    )


def two_tiles(packs):
    tiles = []
    for b in (-1, 0, 1):
        total = None
        for dest, col in ((0, b - 1), (64, 128 + b)):
            place = -1 if col < 0 else (1 if col > 127 else 0)
            local = col - place * TC
            base = dict(TWO)[local]
            for drow, first, last in ((-1, 0, 2), (0, 2, 18), (1, 18, 20)):
                value = rl(packs[(drow, place)], dest + 2 + 16 * drow - base, 1)
                lane = lane_of(value.shape)
                if total is None:
                    total = jnp.zeros(value.shape, F32)
                total = jnp.where((lane >= dest + first) & (lane < dest + last), value, total)
        tiles.append(total)
    return tiles


def tile_inside(b, shape):
    lane = lane_of(shape)
    row = lax.axis_index("row")
    col = lax.axis_index("col")
    local = jnp.where(lane < 64, lane, lane - 64)
    y = row * TR - 2 + local
    x = jnp.where(lane < 64, col * TC - 1 + b, col * TC + TC + b)
    return (y >= 0) & (y < NROW * TR) & (x >= 0) & (x < NCOL * TC) & (local < 20)


def rim_patches(tiles, a):
    return jnp.concatenate([rl(t, -a, 1) for t in tiles], 0).astype(BF16)


def silu_parts(value):
    sigma = jax.nn.sigmoid(value)
    return value * sigma, sigma * (1.0 + value * (1.0 - sigma))


def refine_kernel(
    cv, cvtop, cvbot, n0, n1, n2, n3, n4, n5, n6, n7, pack,
    cot, ctop, cbot, m0, m1, m2, m3, m4, m5, m6, m7, cpack,
    coef, w1, w1f, w2, w2f,
    refined, gpre, gfirst, gsecond, sums,
    cwide, n3x, c3x, h3, gh3, hpre, gmain, s1, s2, rwide,
):
    places = [(-a, -b) for a, b in AROUND]
    row = lax.axis_index("row")
    first = row == 0
    last = row == NROW - 1
    scale, bias, inv, mid = (coef[k] for k in range(4))
    packs = {place: ref[0] for place, ref in zip(places, (n0, n1, n2, n3, n4, n5, n6, n7))}
    packs[(0, 0)] = pack[0]
    cpacks = {place: ref[0].astype(F32) for place, ref in zip(places, (m0, m1, m2, m3, m4, m5, m6, m7))}
    cpacks[(0, 0)] = cpack[0].astype(F32)

    def outer(k):
        return first if k < 2 else last

    def normed_of(value):
        return silu_parts(value * scale + bias)[0]

    ntiles = [
        jnp.where(tile_inside(b - 1, (CH, TC)), normed_of(t), 0.0) for b, t in enumerate(two_tiles(packs))
    ]

    def nrow(k):
        if k < 2:
            return jnp.where(first, 0.0, normed_of(cvtop[k]))
        if k >= 18:
            return jnp.where(last, 0.0, normed_of(cvbot[k - 18]))
        return normed_of(cv[k - 2])

    build_x3(n3x, nrow, ntiles[1], 20, CH)
    ctiles = [
        jnp.where(tile_inside(b - 1, (32, TC)), t, 0.0) for b, t in enumerate(two_tiles(cpacks))
    ]
    cwide[...] = cot[...].astype(F32)

    def crow(k):
        if k < 2:
            return jnp.where(first, 0.0, ctop[k].astype(F32))
        if k >= 18:
            return jnp.where(last, 0.0, cbot[k - 18].astype(F32))
        return strided(cwide, k - 2, 32)

    build_x3(c3x, crow, ctiles[1], 20, 32)

    def both(w_ref, x3, tiles):
        depth = x3.shape[0]
        rim = None
        for a in range(3):
            term = dot(w_ref[:, a * depth : (a + 1) * depth], rim_patches(tiles, a))
            rim = term if rim is None else rim + term
        return rim

    lane = lane_of((64, TC))
    local = jnp.where(lane < 64, lane, lane - 64)
    ypos = row * TR - 1 + local
    col = lax.axis_index("col")
    xpos = jnp.where(lane < 64, col * TC - 1, col * TC + TC)
    rim_in = (ypos >= 0) & (ypos < NROW * TR) & (local < 18) & (xpos >= 0) & (xpos < NCOL * TC)
    rim_h, rim_slope = silu_parts(both(w1, n3x, ntiles))
    rim_g = both(w2f, c3x, ctiles)
    rim_h = jnp.where(rim_in, rim_h, 0.0)
    rim_g = jnp.where(rim_in, rim_g * rim_slope, 0.0)
    for n in range(6):
        hpre[:, n * 384 : (n + 1) * 384] = conv_chunk(w1, n3x, n * 384, 384)
        gmain[:, n * 384 : (n + 1) * 384] = conv_chunk(w2f, c3x, n * 384, 384)

    def edge(k):
        return first if k == 0 else (last if k == 17 else None)

    def hrow(k):
        value, slope = silu_parts(hpre[:, k * TC : (k + 1) * TC])
        grad = gmain[:, k * TC : (k + 1) * TC] * slope
        gone = edge(k)
        if gone is not None:
            value = jnp.where(gone, 0.0, value)
            grad = jnp.where(gone, 0.0, grad)
        gmain[:, k * TC : (k + 1) * TC] = grad
        return value

    build_x3(h3, hrow, rim_h, 18, 64)
    build_x3(gh3, lambda k: gmain[:, k * TC : (k + 1) * TC], rim_g, 18, 64)
    for n in range(4):
        value = conv_chunk(w2, h3, n * 512, 512)
        for j in range(4):
            rwide[pl.ds(n * 4 + j, 32, stride=TR), :] = value[:, j * TC : (j + 1) * TC]
    refined[...] = rwide[...].astype(BF16)
    own = slice(TC, 17 * TC)
    mine = slice(2 * TC, 18 * TC)
    for a in range(3):
        gsecond[:, a * 192 : (a + 1) * 192] = dot_nt(c3x[32:64, mine], h3[:, a * TC : (a + 16) * TC])
        gfirst[:, a * 432 : (a + 1) * 432] = dot_nt(gh3[64:128, own], n3x[:, (a + 1) * TC : (a + 17) * TC])
    s1[...] = jnp.zeros_like(s1)
    s2[...] = jnp.zeros_like(s2)
    for n in range(4):
        value = conv_chunk(w1f, gh3, n * 512, 512)
        for j in range(4):
            y = n * 4 + j
            volume = cv[y]
            grad = value[:, j * TC : (j + 1) * TC] * silu_parts(volume * scale + bias)[1]
            gpre[y] = grad
            s1[...] += grad
            s2[...] += grad * (volume * inv - mid)
    sums[...] = jnp.zeros_like(sums)
    sums[:, 0:CH] = row_sums(s1[...], s2[...])


def correlate_back_kernel(cv, gpre, coef, fw, m, gfw, gm, q, qrim):
    def at_row(y, carry):
        lanes = pl.ds(pl.multiple_of(y * TC, TC), TC)
        grad = coef[0] * gpre[y] + coef[1] + coef[2] * cv[y]
        grad = grad.astype(BF16).astype(F32)
        for a in range(9):
            main, rim = unshear(grad[a * 16 : (a + 1) * 16])
            q[pl.ds(pl.multiple_of((y + a) * TC, TC), TC), lanes] = main.astype(BF16)
            qrim[pl.ds(pl.multiple_of((y + a + 12) * 8, 8), 8), lanes] = rim
        return carry

    qrim[...] = jnp.zeros_like(qrim)
    lax.fori_loop(0, TR, at_row, 0)
    for y in range(TR):
        at = slice(y * TC, (y + 1) * TC)
        value = dot(m[:, y * TC : (y + 9) * TC], q[y * TC : (y + 9) * TC, at])
        value = value + dot(m[:, 24 * TC : 27 * TC], qrim[:, at].astype(BF16))
        gfw[:, at] = (value * 0.0625).astype(BF16)
    for r in range(24):
        at = slice(max(0, r - 8) * TC, (min(15, r) + 1) * TC)
        value = dot_nt(fw[:, at], q[r * TC : (r + 1) * TC, at])
        gm[r] = (value * 0.0625).astype(BF16)
    for k in range(3):
        value = dot_nt(fw[...], qrim[k * TC : (k + 1) * TC, :].astype(BF16))
        gm[24 + k] = (value * 0.0625).astype(BF16)


def return_kernel(off, gm, out, trio, strip, pstrip, ab, be, ab2, be2, pab, pfar, mine, side, lsem, sems, rsems):
    row = lax.axis_index("row")
    col = lax.axis_index("col")
    steps = [(1, 0), (-1, 0), (2, 0), (-2, 0), (0, 1), (0, -1)]
    own = pltpu.make_async_copy(gm, trio.at[1, pl.ds(0, 27)], lsem.at[0])
    own.start()
    for k in range(3):
        trio[k, 27] = jnp.zeros((C, TC), BF16)
    greet(steps)

    def remote(k, src, dst, step):
        return pltpu.make_async_remote_copy(
            src_ref=src,
            dst_ref=dst,
            send_sem=sems.at[k],
            recv_sem=rsems.at[k],
            device_id=device_at(*step),
            device_id_type=MESH,
        )

    stage = [
        remote(0, gm, trio.at[0, pl.ds(0, 27)], (0, 1)),
        remote(1, gm, trio.at[2, pl.ds(0, 27)], (0, -1)),
    ]
    for copy in stage:
        copy.start()
    own.wait()
    for copy in stage:
        copy.wait()
    sources = []
    for k in range(3):
        place = col + k - 1
        there = lax.rem(place + NCOL, NCOL)
        drow = offset_of(off, 0, row, there)
        dcol = offset_of(off, 1, row, there)
        good = (dcol == 1 - k) & (place >= 0) & (place < NCOL)
        sources.append((drow, good))

    def gather(p, carry):
        total = jnp.zeros((C, TC), F32)
        for k, (drow, good) in enumerate(sources):
            j = p - 16 * (drow + 1)
            fits = good & (j >= 0) & (j < 24)
            total = total + trio[k, jnp.where(fits, j, 27)].astype(F32)
        strip[p] = total.astype(BF16)
        return carry

    lax.fori_loop(0, 56, gather, 0)
    for p in range(5):
        total = jnp.zeros((C, TC), F32)
        for k, (drow, good) in enumerate(sources):
            j = p - (drow + 1)
            fits = good & (j >= 0) & (j < 3)
            total = total + trio[k, jnp.where(fits, 24 + j, 27)].astype(F32)
        pstrip[p] = total.astype(BF16)
    stage = [
        remote(2, strip.at[pl.ds(4, TR)], be, (-1, 0)),
        remote(3, strip.at[pl.ds(36, TR)], ab, (1, 0)),
        remote(4, strip.at[pl.ds(0, 4)], be2, (-2, 0)),
        remote(5, strip.at[pl.ds(52, 4)], ab2, (2, 0)),
        remote(6, pstrip.at[pl.ds(1, 1)], pab.at[pl.ds(1, 1)], (-1, 0)),
        remote(7, pstrip.at[pl.ds(3, 1)], pab.at[pl.ds(0, 1)], (1, 0)),
        remote(8, pstrip.at[pl.ds(0, 1)], pfar.at[pl.ds(1, 1)], (-2, 0)),
        remote(9, pstrip.at[pl.ds(4, 1)], pfar.at[pl.ds(0, 1)], (2, 0)),
    ]
    for copy in stage:
        copy.start()
    for copy in stage:
        copy.wait()
    up1, up2 = row >= 1, row >= 2
    down1, down2 = row < NROW - 1, row < NROW - 2
    zero = jnp.zeros((C, TC), F32)

    def only(flag, ref):
        return jnp.where(flag, ref.astype(F32), zero)

    total = pstrip[2].astype(F32) + only(up1, pab[0]) + only(down1, pab[1])
    total = total + only(up2, pfar[0]) + only(down2, pfar[1])
    mine[...] = total.astype(BF16)
    stage = [
        remote(10, mine, side.at[0], (0, 1)),
        remote(11, mine, side.at[1], (0, -1)),
    ]
    for copy in stage:
        copy.start()
    for copy in stage:
        copy.wait()
    lane = lane_of((C, TC))
    left = only(col > 0, side[0])
    right = only(col < NCOL - 1, side[1])
    for y in range(TR):
        total = strip[20 + y].astype(F32) + only(up1, ab[y]) + only(down1, be[y])
        if y < 4:
            total = total + only(up2, ab2[y])
        if y >= 12:
            total = total + only(down2, be2[y - 12])
        total = total + jnp.where(lane < 4, rl(left, -y * 8, 1), 0.0)
        total = total + jnp.where(lane >= 124, rl(right, 124 - (y * 8 + 4), 1), 0.0)
        out[:, y * TC : (y + 1) * TC] = total.astype(BF16)


def give_back(offsets, gm):
    return call(
        return_kernel,
        [sds((C, TR * TC), BF16)],
        [offsets, gm],
        [
            pltpu.VMEM((3, 28, C, TC), BF16),
            pltpu.VMEM((56, C, TC), BF16),
            pltpu.VMEM((5, C, TC), BF16),
            pltpu.VMEM((TR, C, TC), BF16),
            pltpu.VMEM((TR, C, TC), BF16),
            pltpu.VMEM((4, C, TC), BF16),
            pltpu.VMEM((4, C, TC), BF16),
            pltpu.VMEM((2, C, TC), BF16),
            pltpu.VMEM((2, C, TC), BF16),
            pltpu.VMEM((C, TC), BF16),
            pltpu.VMEM((2, C, TC), BF16),
            pltpu.SemaphoreType.DMA((1,)),
            pltpu.SemaphoreType.DMA((12,)),
            pltpu.SemaphoreType.DMA((12,)),
        ],
        in_specs=[sspec(), vspec()],
        collective_id=4,
        has_side_effects=True,
    )[0]


def last_kernel(k, g, top, bottom, p0, p1, p2, p3, p4, p5, w_ref, out, x3, wide):
    packs = dict(zip(PACK_PLACES, (p0, p1, p2, p3, p4, p5)))
    first_row = lax.axis_index("row") == 0
    last_row = lax.axis_index("row") == NROW - 1

    def row(j):
        if j == 0:
            return end_row(top[k], first_row)
        if j == TR + 1:
            return end_row(bottom[k], last_row)
        return g[:, (j - 1) * TC : j * TC].astype(F32)

    build_x3(x3, row, halo_cols(packs, k), TR + 2, C)
    for n in range(4):
        value = conv_chunk(w_ref, x3, n * 512, 512)
        for j in range(4):
            wide[pl.ds(n * 4 + j, C, stride=TR), :] = value[:, j * TC : (j + 1) * TC]
    out[...] = wide[...].astype(BF16)


def weight_kernel(gw, gs, xw, xs, out):
    for a in range(3):
        at = slice(a * TC, (a + 16) * TC)
        for n in range(3):
            part = slice(n * C, (n + 1) * C)
            value = dot_nt(gw[...], xw[part, at]) + dot_nt(gs[...], xs[part, at])
            out[:, a * 768 + n * C : a * 768 + (n + 1) * C] = value


def flip_weight(weight, in_channels):
    out_channels = weight.shape[0]
    return (
        weight.reshape(out_channels, 9, in_channels)[:, ::-1, :]
        .transpose(2, 1, 0)
        .reshape(in_channels, 9 * out_channels)
    )


def spread(vector):
    return jnp.pad(vector.reshape(9, 9), ((0, 0), (0, 7))).reshape(CH)


def gathered(vector):
    return vector.reshape(9, 16)[:, :9].reshape(81)


def across(*vectors):
    return jnp.stack([jnp.broadcast_to(v[:, None], (CH, TC)) for v in vectors])


def body(winter, summer, offsets, feat_weight, bn_gain, bn_shift, w_first, w_second, cotangent):
    w2 = winter.reshape(C * TR, TC)
    s2 = summer.reshape(C * TR, TC)
    c2 = cotangent.reshape(32 * TR, TC)
    flat = offsets.reshape(-1)
    rows, pack, crows, cpack = call(
        edges_kernel,
        [sds((4, C, TC), BF16), sds((2, C, TC), BF16), sds((4, 32, TC), BF16), sds((1, 32, TC), BF16)],
        [w2, s2, c2],
        [pltpu.VMEM((C * TR, TC), F32), pltpu.VMEM((32 * TR, TC), F32)],
    )
    moves = halo_moves(0)
    got = exchange(
        [rows, pack, crows, cpack],
        moves + [(2, 2, 2, (1, 0)), (2, 0, 2, (-1, 0))] + [(3, 0, 1, step) for step in AROUND],
        0,
    )
    halo = got[:8]
    chalo = got[8:]

    def feat(k, x):
        summer_side = k == 1
        out = sds((TR + 1, C, TC), BF16) if summer_side else sds((C, TR * TC), BF16)
        return call(
            functools.partial(feat_kernel, k, summer_side),
            [out, sds((3 * C, 18 * TC), BF16)],
            [x] + halo + [feat_weight],
            [pltpu.VMEM((C * TR, TC), F32)],
        )

    fs, xs = feat(1, s2)
    fw, xw = feat(0, w2)
    m = match(flat, fs)
    cv, cvpack, sums = call(
        correlate_kernel,
        [sds((TR, CH, TC), F32), sds((1, CH, TC), F32), sds((8, 256), F32)],
        [fw, m],
        [
            pltpu.VMEM((24 * TC, C), BF16),
            pltpu.VMEM((3 * TC, C), BF16),
            pltpu.VMEM((3 * TC, TR * TC), F32),
            pltpu.VMEM((CH, TC), F32),
            pltpu.VMEM((CH, TC), F32),
        ],
    )
    got = stats(
        sums,
        [cv, cvpack],
        [(0, 14, 2, (1, 0)), (0, 0, 2, (-1, 0))] + [(1, 0, 1, step) for step in AROUND],
        2,
    )
    sums, vhalo = got[0], got[1:]
    mean = sums[0, :CH] / PIXELS
    inv = lax.rsqrt(sums[1, :CH] / PIXELS - mean * mean + 1e-05)
    gain = spread(bn_gain)
    scale = gain * inv
    coef = across(scale, spread(bn_shift) - mean * scale, inv, mean * inv)
    w1 = jnp.pad(w_first.reshape(64, 9, 9, 9), ((0, 0), (0, 0), (0, 0), (0, 7))).reshape(64, 9 * CH)
    dma = pltpu.SemaphoreType.DMA
    refined, gpre, gfirst, gsecond, gsums = call(
        refine_kernel,
        [
            sds((32 * TR, TC), BF16),
            sds((TR, CH, TC), F32),
            sds((64, 9 * CH), F32),
            sds((32, 576), F32),
            sds((8, 256), F32),
        ],
        [cv] + vhalo + [cvpack] + [c2] + chalo + [cpack]
        + [coef, w1, flip_weight(w1, CH), w_second, flip_weight(w_second, 64)],
        [
            pltpu.VMEM((32 * TR, TC), F32),
            pltpu.VMEM((3 * CH, 20 * TC), BF16),
            pltpu.VMEM((96, 20 * TC), BF16),
            pltpu.VMEM((192, 18 * TC), BF16),
            pltpu.VMEM((192, 18 * TC), BF16),
            pltpu.VMEM((64, 18 * TC), F32),
            pltpu.VMEM((64, 18 * TC), F32),
            pltpu.VMEM((CH, TC), F32),
            pltpu.VMEM((CH, TC), F32),
            pltpu.VMEM((32 * TR, TC), F32),
        ],
    )
    gsums = stats(gsums, [], [], 3)[0]
    grad_shift = gsums[0, :CH]
    grad_gain = gsums[1, :CH]
    slope = -scale * grad_gain / PIXELS
    coef = across(scale, -scale * grad_shift / PIXELS - slope * mean * inv, slope * inv)
    gfw, gm = call(
        correlate_back_kernel,
        [sds((C, TR * TC), BF16), sds((27, C, TC), BF16)],
        [cv, gpre, coef, fw, m],
        [pltpu.VMEM((24 * TC, TR * TC), BF16), pltpu.VMEM((3 * TC, TR * TC), F32)],
    )
    gfs = give_back(flat, gm)
    rows, pack = call(
        edges2_kernel, [sds((4, C, TC), BF16), sds((2, C, TC), BF16)], [gfw, gfs]
    )
    ghalo = exchange([rows, pack], moves, 5)
    flipped = flip_weight(feat_weight, C)

    def last(k, g):
        return call(
            functools.partial(last_kernel, k),
            [sds((C * TR, TC), BF16)],
            [g] + ghalo + [flipped],
            [pltpu.VMEM((3 * C, 18 * TC), BF16), pltpu.VMEM((C * TR, TC), F32)],
        )[0].reshape(C, TR, TC)

    grad_feat = call(weight_kernel, [sds((C, 9 * C), F32)], [gfw, gfs, xw, xs])[0]
    sums3 = lax.psum((grad_feat, gfirst, gsecond), ("row", "col"))
    grad_winter = last(0, gfw)
    grad_summer = last(1, gfs)
    return (
        refined.reshape(32, TR, TC),
        grad_winter,
        grad_summer,
        sums3[0],
        sums3[1].reshape(64, 9, 9, 16)[:, :, :, :9].reshape(64, 729),
        sums3[2],
        gathered(grad_gain),
        gathered(grad_shift),
    )


def solution(mesh):
    tile = P(None, "row", "col")
    return jax.shard_map(
        body,
        mesh=mesh,
        in_specs=(tile, tile, P(), P(), P(), P(), P(), P(), tile),
        out_specs=(tile, tile, tile, P(), P(), P(), P(), P()),
        check_vma=False,
    )
```

time: 1200 us -> 457 us (0.38); the launches traced: 1180 us -> 449 us
  local copies, waits for them, and re-layouts: 469 us -> 17.1 us
  Pallas kernels: 0 us -> 297 us
  waiting for transfers between devices: 272 us -> 118 us
  blocking collectives: 140 us -> 0 us
  matrix products: 114 us -> 0 us
  starting transfers between devices: 105 us -> 0.04 us
  other arithmetic: 52.3 us -> 2.28 us
  between operations: 26.7 us -> 14.5 us
    pallas_call x0 -> x16, Pallas kernels: none -> 297 us  [call(): pl.pallas_call(kernel, out_shape=outs, in_specs=in_specs or [vspec() for...]
    reshape x41 -> x13, local copies, waits for them, and re-layouts: 181 us -> 7.5 us  [the longest x3 3.27 us: flip_weight(): return weight.reshape(out_channels, 9, in_channels)[:, ::-1, :].transpose...]
    ppermute x40 -> x0, waiting for transfers between devices: 150 us -> none  [the longest x14 110 us: extended(): lax.ppermute(lax.slice_in_dim(block, 0, width, axis=dim), axis, backward)]
    psum x2 -> x0, blocking collectives: 140 us -> none  [the longest x1 72.3 us: body(): lax.psum((jnp.sum(grad_pre, axis=(1, 2)), jnp.sum(grad_pre * centred, axi...]
    dot_general x39 -> x0, matrix products: 114 us -> none  [the longest x8 33.4 us: conv_local(): jnp.dot(weight, patches(padded, height, wide_cols), preferred_element_typ...]
    ppermute x40 -> x0, starting transfers between devices: 105 us -> none  [the longest x14 48.5 us: extended(): lax.ppermute(lax.slice_in_dim(block, block.shape[dim] - width, None, axis...]
    concatenate x21 -> x0, local copies, waits for them, and re-layouts: 94.9 us -> none  [the longest x9 51.2 us: patches(): jnp.concatenate([padded[:, shift_row:shift_row + height, shift_col:shift_...]
    unnamed x217 -> x22, local copies, waits for them, and re-layouts: 87.8 us -> 5.59 us
  transfers between devices with their start and end apart: 41 -> 1, of which waited for: 15 -> 1; matrix products, arithmetic and copies ran while one was open for 29% -> 1% of each run, Pallas kernels for 0% -> 8%
where the time goes in v1:
time: 457 us; the launch traced here: 449 us
  Pallas kernels  297 us (65%)
  waiting for transfers between devices  118 us (26%)
  local copies, waits for them, and re-layouts  17.1 us (4%)
  between operations  14.5 us (3%)
    pallas_call x16, Pallas kernels, call(): pl.pallas_call(kernel, out_shape=outs, in_specs=in_specs or [vspec() for...  297 us
    psum x1, waiting for transfers between devices, body(): sums3 = lax.psum((grad_feat, gfirst, gsecond), ('row', 'col'))  118 us
  transfers between devices with their start and end apart: 1, of which 1 were waited for; matrix products, arithmetic and copies ran while one was open for 1% of the time, Pallas kernels for 8%

profile of v1, /device:TPU:1, one launch (start us, length us, event | category | flops | bytes accessed | tf_op | source)
XLA Modules:
  0.0 448.8 jit_solution(8183233583213779990)
XLA Ops:
  7.2 5.0 %shard_map.152 = (bf16[4,256,128]{2,1,0:T(8,128)(2,1)}, bf16[2,256,128]{2,1,0:T(8,128)(2,1)}, bf16[4,32,128]{2,1,0:T(8,128)(2,1)}, bf16[1,32,128]{2,1,0:T(8,128)(2,1)}) custom-call(bf16[4096,128]{1,0:T(8,128)(2,1)} %bitcast.33, bf16[4096,128]{1,0:T(8,128)(2,1)} %bitcast.31, bf16[512,128]{1,0:T(8,128)(2,1)} %bitcast.42), custom_call_target="tpu_custom_call" | custom-call | tf_op jit(solution)/shard_map/pallas_call | solution.py:42
  12.2 20.5 %shard_map.153 = (bf16[2,256,128]{2,1,0:T(8,128)(2,1)}, bf16[2,256,128]{2,1,0:T(8,128)(2,1)}, bf16[2,256,128]{2,1,0:T(8,128)(2,1)}, bf16[2,256,128]{2,1,0:T(8,12...) custom-call(bf16[4,256,128]{2,1,0:T(8,128)(2,1)} %get-tuple-element., ...), custom_call_target="tpu_custom_call" | custom-call | tf_op jit(solution)/shard_map/pallas_call | solution.py:42
  32.7 8.0 %shard_map.155 = (bf16[17,256,128]{2,1,0:T(8,128)(2,1)}, bf16[768,2304]{1,0:T(8,128)(2,1)}) custom-call(bf16[4096,128]{1,0:T(8,128)(2,1)} %bitcast.32, bf16[2,256,128]{2,1,0:T(8,128)(2,1)} %get-tuple-element.69.top, bf16[2,256,128]{2,1,0:T(8,128)(2,1)} %get-tuple-element.70.bottom, bf16[2,256,128]{2,1,0:T(8,128)(2,1)} %get-tuple-element.71.p0, ...), custom_call_target="tpu_custom_call" | custom-call | tf_op jit(solution)/shard_map/pallas_call | solution.py:42
  40.7 6.3 %shard_map.154 = (bf16[256,2048]{1,0:T(8,128)(2,1)}, bf16[768,2304]{1,0:T(8,128)(2,1)}) custom-call(bf16[4096,128]{1,0:T(8,128)(2,1)} %bitcast.34, bf16[2,256,128]{2,1,0:T(8,128)(2,1)} %get-tuple-element.69.top, bf16[2,256,128]{2,1,0:T(8,128)(2,1)} %get-tuple-element.70.bottom, bf16[2,256,128]{2,1,0:T(8,128)(2,1)} %get-tuple-element.71.p0, ...), custom_call_target="tpu_custom_call" | custom-call | tf_op jit(solution)/shard_map/pallas_call | solution.py:42
  47.7 74.3 %shard_map.156.m = bf16[256,3456]{1,0:T(8,128)(2,1)} custom-call(s32[256]{0:T(256)} %reshape.89.off, bf16[17,256,128]{2,1,0:T(8,128)(2,1)} %get-tuple-element.78.fp), custom_call_target="tpu_custom_call" | custom-call | tf_op jit(solution)/shard_map/pallas_call | solution.py:42
  122.1 9.6 %shard_map.157 = (f32[16,144,128]{2,1,0:T(8,128)}, f32[1,144,128]{2,1,0:T(8,128)}, f32[8,256]{1,0:T(8,128)}) custom-call(bf16[256,2048]{1,0:T(8,128)(2,1)} %get-tuple-element.77.fw, bf16[256,3456]{1,0:T(8,128)(2,1)} %shard_map.156.m), custom_call_target="tpu_custom_call" | custom-call | tf_op jit(solution)/shard_map/pallas_call | solution.py:42
  131.7 18.6 %shard_map.158 = (f32[8,256]{1,0:T(8,128)}, f32[2,144,128]{2,1,0:T(8,128)}, f32[2,144,128]{2,1,0:T(8,128)}, f32[1,144,128]{2,1,0:T(8,128)}, f32[1,144,128]{2,1,0...) custom-call(f32[8,256]{1,0:T(8,128)} %get-tuple-element.80.refs_0_, ...), custom_call_target="tpu_custom_call" | custom-call | tf_op jit(solution)/shard_map/pallas_call | solution.py:42
  152.1 0.8 copy.25.w1f
  152.9 0.8 copy.24.w1
  155.8 8.6 %shard_map.159 = (bf16[512,128]{1,0:T(8,128)(2,1)}, f32[16,144,128]{2,1,0:T(8,128)}, f32[64,1296]{1,0:T(8,128)}, f32[32,576]{1,0:T(8,128)}, f32[8,256]{1,0:T(8,128)}) custom-call(f32[16,144,128]{2,1,0:T(8,128)} %get-tuple-element.79.refs_1_.cv, f32[2,144,128]{2,1,0:T(8,128)} %get-tuple-element.82.cvtop, f32[2,144,128]{2,1,0:T(8,128)} %get-tuple-element.83.cvbot, ...), custom_call_target="tpu_custom_call" | custom-call | tf_op jit(solution)/shard_map/pallas_call | solution.py:42
  164.5 12.9 %shard_map.160 = f32[8,256]{1,0:T(8,128)} custom-call(f32[8,256]{1,0:T(8,128)} %get-tuple-element.105.refs_0_), custom_call_target="tpu_custom_call" | custom-call | tf_op jit(solution)/shard_map/pallas_call | solution.py:42
  179.0 14.0 %shard_map.161 = (bf16[256,2048]{1,0:T(8,128)(2,1)}, bf16[27,256,128]{2,1,0:T(8,128)(2,1)}) custom-call(f32[16,144,128]{2,1,0:T(8,128)} %get-tuple-element.79.refs_1_.cv, f32[16,144,128]{2,1,0:T(8,128)} %get-tuple-element.104.gpre, f32[3,144,128]{2,1,0:T(8,128)} %pad_maximum_fusion.1.coef, bf16[256,2048]{1,0:T(8,128)(2,1)} %get-tuple-element.77.fw, ...), custom_call_target="tpu_custom_call" | custom-call | tf_op jit(solution)/shard_map/pallas_call | solution.py:42
  193.0 75.0 %shard_map.162.s_ref.g.gs = bf16[256,2048]{1,0:T(8,128)(2,1)} custom-call(s32[256]{0:T(256)} %reshape.89.off, bf16[27,256,128]{2,1,0:T(8,128)(2,1)} %get-tuple-element.107.gm), custom_call_target="tpu_custom_call" | custom-call | tf_op jit(solution)/shard_map/pallas_call | solution.py:42
  268.0 1.1 copy.31
  269.1 10.2 %shard_map.167 = f32[256,2304]{1,0:T(8,128)} custom-call(bf16[256,2048]{1,0:T(8,128)(2,1)} %get-tuple-element.106.w_ref.g.gw, bf16[256,2048]{1,0:T(8,128)(2,1)} %shard_map.162.s_ref.g.gs, bf16[768,2304]{1,0:T(8,128)(2,1)} %get-tuple-element.118.xw, bf16[768,2304]{1,0:T(8,128)(2,1)} %get-tuple-element.119.xs), custom_call_target="tpu_custom_call" | custom-call | tf_op jit(solution)/shard_map/pallas_call | solution.py:42
  279.3 3.6 shard_map.163
  284.3 1.7 copy.29.w_ref
  286.1 17.4 %shard_map.164 = (bf16[2,256,128]{2,1,0:T(8,128)(2,1)}, bf16[2,256,128]{2,1,0:T(8,128)(2,1)}, bf16[2,256,128]{2,1,0:T(8,128)(2,1)}, bf16[2,256,128]{2,1,0:T(8,12...) custom-call(bf16[4,256,128]{2,1,0:T(8,128)(2,1)} %get-tuple-element., ...), custom_call_target="tpu_custom_call" | custom-call | tf_op jit(solution)/shard_map/pallas_call | solution.py:42
  303.5 6.5 %shard_map.166 = bf16[4096,128]{1,0:T(8,128)(2,1)} custom-call(bf16[256,2048]{1,0:T(8,128)(2,1)} %shard_map.162.s_ref.g.gs, bf16[2,256,128]{2,1,0:T(8,128)(2,1)} %get-tuple-element.110.top, bf16[2,256,128]{2,1,0:T(8,128)(2,1)} %get-tuple-element.111.bottom, bf16[2,256,128]{2,1,0:T(8,128)(2,1)} %get-tuple-element.112.p0, ...), custom_call_target="tpu_custom_call" | custom-call | tf_op jit(solution)/shard_map/pallas_call | solution.py:42
  309.9 6.4 %shard_map.165 = bf16[4096,128]{1,0:T(8,128)(2,1)} custom-call(bf16[256,2048]{1,0:T(8,128)(2,1)} %get-tuple-element.106.w_ref.g.gw, bf16[2,256,128]{2,1,0:T(8,128)(2,1)} %get-tuple-element.110.top, bf16[2,256,128]{2,1,0:T(8,128)(2,1)} %get-tuple-element.111.bottom, bf16[2,256,128]{2,1,0:T(8,128)(2,1)} %get-tuple-element.112.p0, ...), custom_call_target="tpu_custom_call" | custom-call | tf_op jit(solution)/shard_map/pallas_call | solution.py:42
  317.7 118.2 %all-reduce.6.cloned.1.call-done = (f32[256,2304]{1,0:T(8,128)}, f32[64,9,9,16]{0,3,2,1:T(8,128)}, f32[32,576]{1,0:T(8,128)}) async-done(((f32[256,2304]{1,0:T(8,128)}, f32[64,9,9,16]{0,3,2,1:T(8,128)}, f32[32,576]{1,0:T(8,128)}), (f32[256,2304]{1,0:T(8,128)}, f32[64,9,9,16]{0,3,2,1:T(8,128)}, f32[32,576]{1,0:T(8,128)})) %all-reduce.6.cloned.1.call-update) | async-done | bytes 2764816 | tf_op jit(solution)/shard_map/psum | solution.py:1005
  435.9 1.1 reshape.105
  437.0 0.8 copy.32
  437.8 3.3 copy.36
  (56 shorter events, 9.6 us)
Async XLA Ops:
  7.2 428.7 %all-reduce.6.cloned.1.call-start = ((), (), s32[]{:S(2)}) async-start(), calls=%async_computation | async-start | bytes 6209536 | tf_op jit(solution)/shard_map/psum | solution.py:1005
  40.7 6.3 %copy-start.5 = (s32[2,16,8]{1,2,0:T(8,128)S(1)}, s32[2,16,8]{1,2,0:T(8,128)}, u32[]{:S(2)}) copy-start(s32[2,16,8]{1,2,0:T(8,128)} %param.11) | copy-start | bytes 3076
  131.7 19.4 %copy-start.6 = (f32[81]{0:T(128)S(1)}, f32[81]{0:T(128)}, u32[]{:S(2)}) copy-start(f32[81]{0:T(128)} %param.13) | copy-start | bytes 976
  131.7 19.6 %copy-start.7 = (f32[81]{0:T(128)S(1)}, f32[81]{0:T(128)}, u32[]{:S(2)}) copy-start(f32[81]{0:T(128)} %param.14) | copy-start | bytes 976
  131.7 19.8 %copy-start.3 = (bf16[64,729]{1,0:T(8,128)(2,1)S(1)}, bf16[64,729]{1,0:T(8,128)(2,1)}, u32[]{:S(2)}) copy-start(bf16[64,729]{1,0:T(8,128)(2,1)} %param.15) | copy-start | bytes 279940
  151.8 1.9 copy-start.2
  193.0 75.0 %copy-start.1 = (f32[64,1296]{1,0:T(8,128)S(1)}, f32[64,1296]{1,0:T(8,128)}, u32[]{:S(2)}) copy-start(f32[64,1296]{1,0:T(8,128)} %get-tuple-element.120) | copy-start | bytes 995332
  279.3 3.6 copy-start
  437.8 3.3 copy-start.4
Sparse Core Ops, SparseCore 0:
  279.5 156.3 all-reduce.5
